TPU v7x, 1024 devices: a whole 8x8x8 slice. The times are simulated.
1024 devices in a mesh: dp: 64 (over z, y), expert: 16 (over x, core).
Axes of the slice: x: 8, y: 8, z: 8, core: 2. Of those that a mesh axis runs over, the one named last changes fastest.
Arguments:
- tokens: bfloat16 [131072, 1024], P(('dp', 'expert')), may hold values from -6 to 6
- route_ids: int32 [131072, 1], P(('dp', 'expert')), may hold values from 0 to 15; in each aligned block of 128 rows (0 to 127, 128 to 255, ...) at most 12 rows name the same one
- route_weight: float32 [131072, 1], P(('dp', 'expert')), may hold values from 0.02 to 0.5
- w_gate_up: bfloat16 [16, 1024, 768], P('expert'), may hold values from -0.1875 to 0.1875
- w_down: bfloat16 [16, 384, 1024], P('expert'), may hold values from -0.3125 to 0.3125
- out_grad: bfloat16 [131072, 1024], P(('dp', 'expert')), may hold values from -6 to 6
Outputs:
- mixed: bfloat16 [131072, 1024], P(('dp', 'expert'))
- token_grad: bfloat16 [131072, 1024], P(('dp', 'expert'))
- route_weight_grad: float32 [131072, 1], P(('dp', 'expert'))
- weight_grad: float32 [16, 1024, 1152], P('expert', 'dp')
Inputs may be any that keep to these rules, and one draw needn't show every extreme that they name: `route_ids`: among the 128 rows of one device (aligned blocks), no expert is named by more than 12 rows, a bound that some block reaches; a row names 1 different experts.
All inputs are finite; a program needn't handle non-finite values.
Results may differ from a plain program's by a relative error of at most 0.0057.
Values may be sent and summed in bfloat16 or wider, within the bound.
A program may use at most 32 MiB of HBM per device.

v0:
```python
import jax
import jax.numpy as jnp
from jax import lax
from jax.sharding import PartitionSpec as P


def slot_table(route_ids, experts, capacity):
    count, top = route_ids.shape
    flat_ids = route_ids.reshape(count * top)
    onehot = (flat_ids[:, None] == jnp.arange(experts, dtype=jnp.int32)[None, :]).astype(jnp.int32)
    before = jnp.cumsum(onehot, axis=0) - onehot
    position = jnp.sum(before * onehot, axis=1)
    slot = flat_ids * capacity + position
    placed = jnp.arange(experts * capacity, dtype=jnp.int32)[:, None] == slot[None, :]
    return placed.astype(jnp.bfloat16)


def contract_rows(left, right):
    return lax.dot_general(
        left, right, (((0,), (0,)), ((), ())), preferred_element_type=jnp.float32
    )


def on_device(tokens, route_ids, route_weight, w_gate_up, w_down, out_grad):
    experts = lax.axis_size("expert")
    count, top = route_ids.shape
    width = tokens.shape[1]
    hidden = w_down.shape[1]
    capacity = 3 * count * top // (2 * experts)
    slot_rows = experts * capacity
    placed = slot_table(route_ids, experts, capacity)
    by_token = jnp.sum(placed.astype(jnp.float32).reshape(slot_rows, count, top), axis=2).astype(
        jnp.bfloat16
    )
    outgoing = jnp.dot(by_token, tokens, preferred_element_type=jnp.float32).astype(jnp.bfloat16)
    gate_up = w_gate_up[0]
    down = w_down[0]
    arrived = lax.all_to_all(
        outgoing.reshape(experts, capacity, width),
        "expert",
        split_axis=0,
        concat_axis=0,
        tiled=True,
    )
    items = arrived.shape[1]
    rows_in = arrived.reshape(experts * items, width)
    pre_in = jnp.dot(rows_in, gate_up, preferred_element_type=jnp.float32)
    act_in = (jax.nn.silu(pre_in[:, :hidden]) * pre_in[:, hidden:]).astype(jnp.bfloat16)
    result = jnp.dot(act_in, down, preferred_element_type=jnp.float32).astype(jnp.bfloat16)
    back = lax.all_to_all(
        result.reshape(experts, items, width), "expert", split_axis=0, concat_axis=0, tiled=True
    )
    returned = back.reshape(slot_rows, width)
    rows = arrived.reshape(slot_rows, width)
    pre = pre_in.reshape(experts, items, 2 * hidden).reshape(slot_rows, 2 * hidden)
    copy_out = contract_rows(placed, returned).reshape(count, top, width)
    mixed = jnp.einsum("tk,tkd->td", route_weight, copy_out).astype(jnp.bfloat16)
    grad_full = out_grad.astype(jnp.float32)
    route_weight_grad = jnp.einsum("td,tkd->tk", grad_full, copy_out)
    copy_grad = (
        (route_weight[:, :, None] * grad_full[:, None, :])
        .astype(jnp.bfloat16)
        .reshape(count * top, width)
    )
    outgoing_grad = jnp.dot(placed, copy_grad, preferred_element_type=jnp.float32).astype(
        jnp.bfloat16
    )
    arrived_grad = lax.all_to_all(
        outgoing_grad.reshape(experts, capacity, width),
        "expert",
        split_axis=0,
        concat_axis=0,
        tiled=True,
    ).reshape(slot_rows, width)
    gate_pre = pre[:, :hidden]
    up_pre = pre[:, hidden:]
    sig = jax.nn.sigmoid(gate_pre)
    silu_gate = gate_pre * sig
    act = (silu_gate * up_pre).astype(jnp.bfloat16)
    d_act = lax.dot_general(
        arrived_grad, down, (((1,), (1,)), ((), ())), preferred_element_type=jnp.float32
    )
    d_gate = d_act * up_pre * sig * (1.0 + gate_pre * (1.0 - sig))
    d_up = d_act * silu_gate
    d_pre = jnp.concatenate([d_gate, d_up], axis=1).astype(jnp.bfloat16)
    rows_grad = lax.dot_general(
        d_pre, gate_up, (((1,), (1,)), ((), ())), preferred_element_type=jnp.float32
    ).astype(jnp.bfloat16)
    back_grad = lax.all_to_all(
        rows_grad.reshape(experts, capacity, width),
        "expert",
        split_axis=0,
        concat_axis=0,
        tiled=True,
    )
    copy_dx = contract_rows(placed, back_grad.reshape(slot_rows, width)).reshape(count, top, width)
    token_grad = jnp.sum(copy_dx, axis=1).astype(jnp.bfloat16)
    weight_grad = lax.psum_scatter(
        jnp.concatenate([contract_rows(rows, d_pre), contract_rows(arrived_grad, act)], axis=1),
        "dp",
        scatter_dimension=0,
        tiled=True,
    )
    return (mixed, token_grad, route_weight_grad, weight_grad[None])


def solution(mesh):
    placed = (
        P(("dp", "expert"), None),
        P(("dp", "expert"), None),
        P(("dp", "expert"), None),
        P("expert", None, None),
        P("expert", None, None),
        P(("dp", "expert"), None),
    )
    return jax.shard_map(
        on_device,
        mesh=mesh,
        in_specs=placed,
        out_specs=(
            P(("dp", "expert"), None),
            P(("dp", "expert"), None),
            P(("dp", "expert"), None),
            P("expert", "dp", None),
        ),
        check_vma=False,
    )
```

profile of v0, /device:TPU:1, one launch (start us, length us, event | category | flops | bytes accessed | tf_op | source)
XLA Modules:
  0.0 262.7 jit_solution(17733588387376335603)
XLA Ops:
  7.2 0.9 fusion.17
  9.7 1.2 convolution_convert_fusion.2
  11.0 0.9 reshape.78
  11.8 17.5 %all-to-all-start = ((bf16[16,12,1024]{2,1,0:T(8,128)(2,1)}), bf16[16,12,1024]{2,1,0:T(8,128)(2,1)S(1)}, u32[]{:S(2)}, u32[]{:S(2)}) async-start(bf16[16,12,1024]{2,1,0:T(8,128)(2,1)} %reshape.78), calls=%async_computation | async-start | bytes 1048576 | tf_op jit(solution)/shard_map/all_to_all | solution.py:38
  29.7 0.9 reshape.83
  30.6 16.1 %all-to-all-done = bf16[16,12,1024]{2,1,0:T(8,128)(2,1)S(1)} async-done(((bf16[16,12,1024]{2,1,0:T(8,128)(2,1)}), bf16[16,12,1024]{2,1,0:T(8,128)(2,1)S(1)}, u32[]{:S(2)}, u32[]{:S(2)}) %all-to-all-start) | async-done | bytes 393248 | tf_op jit(solution)/shard_map/all_to_all | solution.py:38
  46.7 3.5 %all-to-all-start.2 = ((bf16[16,12,1024]{2,1,0:T(8,128)(2,1)}), bf16[16,12,1024]{2,1,0:T(8,128)(2,1)S(1)}, u32[]{:S(2)}, u32[]{:S(2)}) async-start(bf16[16,12,1024]{2,1,0:T(8,128)(2,1)} %reshape.83), calls=%async_computation.2 | async-start | bytes 1048576 | tf_op jit(solution)/shard_map/all_to_all | solution.py:68
  50.3 1.3 fusion.2
  51.6 15.2 %all-to-all-done.2 = bf16[16,12,1024]{2,1,0:T(8,128)(2,1)S(1)} async-done(((bf16[16,12,1024]{2,1,0:T(8,128)(2,1)}), bf16[16,12,1024]{2,1,0:T(8,128)(2,1)S(1)}, u32[]{:S(2)}, u32[]{:S(2)}) %all-to-all-start.2) | async-done | bytes 393248 | tf_op jit(solution)/shard_map/all_to_all | solution.py:68
  67.0 1.8 multiply_convert_fusion.2
  70.0 2.5 pad_maximum_fusion
  73.3 0.9 reshape.85
  74.2 3.5 %all-to-all-start.3 = ((bf16[16,12,1024]{2,1,0:T(8,128)(2,1)}), bf16[16,12,1024]{2,1,0:T(8,128)(2,1)S(1)}, u32[]{:S(2)}, u32[]{:S(2)}) async-start(bf16[16,12,1024]{2,1,0:T(8,128)(2,1)} %reshape.85), calls=%async_computation.3 | async-start | bytes 1048576 | tf_op jit(solution)/shard_map/all_to_all | solution.py:89
  77.6 1.3 convolution_convert_fusion.1
  78.9 0.9 reshape.80
  79.8 14.6 %all-to-all-done.3 = bf16[16,12,1024]{2,1,0:T(8,128)(2,1)S(1)} async-done(((bf16[16,12,1024]{2,1,0:T(8,128)(2,1)}), bf16[16,12,1024]{2,1,0:T(8,128)(2,1)S(1)}, u32[]{:S(2)}, u32[]{:S(2)}) %all-to-all-start.3) | async-done | bytes 393248 | tf_op jit(solution)/shard_map/all_to_all | solution.py:89
  94.4 3.5 %all-to-all-start.1 = ((bf16[16,12,1024]{2,1,0:T(8,128)(2,1)}), bf16[16,12,1024]{2,1,0:T(8,128)(2,1)S(1)}, u32[]{:S(2)}, u32[]{:S(2)}) async-start(bf16[16,12,1024]{2,1,0:T(8,128)(2,1)} %reshape.80), calls=%async_computation.1 | async-start | bytes 1048576 | tf_op jit(solution)/shard_map/all_to_all | solution.py:50
  97.9 1.3 dynamic-slice
  99.9 14.7 %all-to-all-done.1 = bf16[16,12,1024]{2,1,0:T(8,128)(2,1)S(1)} async-done(((bf16[16,12,1024]{2,1,0:T(8,128)(2,1)}), bf16[16,12,1024]{2,1,0:T(8,128)(2,1)S(1)}, u32[]{:S(2)}, u32[]{:S(2)}) %all-to-all-start.1) | async-done | bytes 393248 | tf_op jit(solution)/shard_map/all_to_all | solution.py:50
  114.7 1.0 convolution_convert_fusion.3
  115.7 1.6 fusion.11
  117.3 136.5 %all-reduce.3.cloned.1.call-done = f32[1024,1152]{0,1:T(8,128)} async-done(((f32[1024,1152]{0,1:T(8,128)}), f32[1024,1152]{0,1:T(8,128)}) %all-reduce.3.cloned.1.call-update) | async-done | bytes 4718608
  253.8 1.3 dynamic-slice_bitcast_fusion
  255.0 0.8 copy.12
  (23 shorter events, 4.4 us)
Async XLA Ops:
  7.2 43.2 %copy-start = (bf16[1,1024,768]{2,1,0:T(8,128)(2,1)S(1)}, bf16[1,1024,768]{2,1,0:T(8,128)(2,1)}, u32[]{:S(2)}) copy-start(bf16[1,1024,768]{2,1,0:T(8,128)(2,1)} %param.9) | copy-start | bytes 4718596
  7.2 22.2 %copy-start.4 = (f32[128,1]{0,1:T(1,128)S(1)}, f32[128,1]{0,1:T(1,128)}, u32[]{:S(2)}) copy-start(f32[128,1]{0,1:T(1,128)} %param.8) | copy-start | bytes 1540
  7.2 22.2 %copy-start.1 = (bf16[128,1024]{1,0:T(8,128)(2,1)S(1)}, bf16[128,1024]{1,0:T(8,128)(2,1)}, u32[]{:S(2)}) copy-start(bf16[128,1024]{1,0:T(8,128)(2,1)} %param.11) | copy-start | bytes 786436
  11.8 34.9 %all-to-all-start = ((bf16[16,12,1024]{2,1,0:T(8,128)(2,1)}), bf16[16,12,1024]{2,1,0:T(8,128)(2,1)S(1)}, u32[]{:S(2)}, u32[]{:S(2)}) async-start(bf16[16,12,1024]{2,1,0:T(8,128)(2,1)} %reshape.78), calls=%async_computation | async-start | bytes 1048576 | tf_op jit(solution)/shard_map/all_to_all | solution.py:38
  46.7 20.2 %all-to-all-start.2 = ((bf16[16,12,1024]{2,1,0:T(8,128)(2,1)}), bf16[16,12,1024]{2,1,0:T(8,128)(2,1)S(1)}, u32[]{:S(2)}, u32[]{:S(2)}) async-start(bf16[16,12,1024]{2,1,0:T(8,128)(2,1)} %reshape.83), calls=%async_computation.2 | async-start | bytes 1048576 | tf_op jit(solution)/shard_map/all_to_all | solution.py:68
  50.2 203.6 %all-reduce.3.cloned.1.call-start = ((), (), s32[]{:S(2)}) async-start(), calls=%async_computation.4 | async-start | bytes 9437184
  68.7 0.7 copy-start.3
  72.6 5.0 %copy-start.2 = (bf16[1,384,1024]{2,1,0:T(8,128)(2,1)S(1)}, bf16[1,384,1024]{2,1,0:T(8,128)(2,1)}, u32[]{:S(2)}) copy-start(bf16[1,384,1024]{2,1,0:T(8,128)(2,1)} %param.10) | copy-start | bytes 2359300
  74.2 20.2 %all-to-all-start.3 = ((bf16[16,12,1024]{2,1,0:T(8,128)(2,1)}), bf16[16,12,1024]{2,1,0:T(8,128)(2,1)S(1)}, u32[]{:S(2)}, u32[]{:S(2)}) async-start(bf16[16,12,1024]{2,1,0:T(8,128)(2,1)} %reshape.85), calls=%async_computation.3 | async-start | bytes 1048576 | tf_op jit(solution)/shard_map/all_to_all | solution.py:89
  94.4 20.2 %all-to-all-start.1 = ((bf16[16,12,1024]{2,1,0:T(8,128)(2,1)}), bf16[16,12,1024]{2,1,0:T(8,128)(2,1)S(1)}, u32[]{:S(2)}, u32[]{:S(2)}) async-start(bf16[16,12,1024]{2,1,0:T(8,128)(2,1)} %reshape.80), calls=%async_computation.1 | async-start | bytes 1048576 | tf_op jit(solution)/shard_map/all_to_all | solution.py:50
Sparse Core Ops, SparseCore 0:
  72.7 180.9 all-reduce.2
where the time goes:
time: 266 us; the launch traced here: 263 us
  waiting for transfers between devices  197 us (74%)
  starting transfers between devices  28 us (11%)
  between operations  14.9 us (6%)
  matrix products  10.1 us (4%)
  local copies, waits for them, and re-layouts  7.52 us (3%)
  other arithmetic  5.08 us (2%)
    unnamed x2, waiting for transfers between devices  137 us
    all_to_all x1, starting transfers between devices, on_device(): lax.all_to_all(outgoing.reshape(experts, capacity, width), 'expert', spli...  17.5 us
    all_to_all x1, waiting for transfers between devices, on_device(): lax.all_to_all(outgoing.reshape(experts, capacity, width), 'expert', spli...  16.1 us
    all_to_all x1, waiting for transfers between devices, on_device(): lax.all_to_all(outgoing_grad.reshape(experts, capacity, width), 'expert',...  15.2 us
    all_to_all x1, waiting for transfers between devices, on_device(): lax.all_to_all(result.reshape(experts, items, width), 'expert', split_axi...  14.7 us
    all_to_all x1, waiting for transfers between devices, on_device(): lax.all_to_all(rows_grad.reshape(experts, capacity, width), 'expert', spl...  14.6 us
  transfers between devices with their start and end apart: 5, of which 5 were waited for; matrix products, arithmetic and copies ran while one was open for 4% of the time, Pallas kernels for 0%

commit v1 on v0

v1 whole, which is shorter than its diff:
```python
import functools

import jax
import jax.numpy as jnp
from jax import lax
from jax.experimental import pallas as pl
from jax.experimental.pallas import tpu as pltpu
from jax.sharding import PartitionSpec as P

MESH = pl.DeviceIdType.MESH
BF16, F32, I32 = jnp.bfloat16, jnp.float32, jnp.int32
CAP = 12
BLOCKS = 4
CUT = 256
MSG = CAP * BLOCKS
GROUP = 4 * MSG
CHIPS = (0, 1, 7, 2, 6, 3, 5, 4)
PLACE = {k: i for i, k in enumerate(CHIPS)}
FAR_FIRST = (14, 15, 12, 13, 10, 11, 8, 9, 6, 7, 4, 5, 2, 3, 1)
NT = (((1,), (1,)), ((), ()))
TN = (((0,), (0,)), ((), ()))


def mirror(slot):
    return 2 * PLACE[(8 - CHIPS[slot // 2]) % 8] + slot % 2


def rows(at, n):
    return pl.ds(at * n, n)


def dot(a, b, dims=(((1,), (0,)), ((), ()))):
    return lax.dot_general(a, b, dims, preferred_element_type=F32)


def kernel(
    ids_ref, wt_ref, tok_hbm, grad_hbm, gu_hbm, down_hbm,
    mixed_ref, tgrad_ref, rwg_ref, wgrad_ref,
    tok, grad, gu, down, spread, gather, perm,
    snd_t, snd_g, rcv_t, rcv_g, xs, gs, p1, p2, act, dpre,
    out_r, out_d, ret_r, ret_d, part, own, got,
    ld_sem, t_ss, t_rs, g_ss, g_rs, r_ss, r_rs, d_ss, d_rs,
    ft_ss, ft_rs, fg_ss, fg_rs, w_ss, w_rs,
):
    dp, ex = lax.axis_index("dp"), lax.axis_index("expert")
    y, z = lax.rem(dp, 8), lax.div(dp, 8)
    x, core = lax.div(ex, 2), lax.rem(ex, 2)

    def expert_at(slot):
        chip = lax.rem(x + CHIPS[slot // 2], 8)
        return {"expert": chip * 2 + (core if slot % 2 == 0 else 1 - core)}

    def dp_at(yy, zz):
        return {"dp": zz * 8 + yy}

    y0, z0 = y + 1 - 2 * lax.rem(y, 2), z + 1 - 2 * lax.rem(z, 2)
    y1, z1 = lax.rem(y + 7 + 2 * lax.rem(y, 2), 8), lax.rem(z + 7 + 2 * lax.rem(z, 2), 8)
    quads = (
        (dp_at(y0, z), dp_at(y, z0), dp_at(y0, z0)),
        (dp_at(y1, z), dp_at(y, z1), dp_at(y1, z1)),
    )

    def peer(m):
        return lax.rem(y + 2 * (m % 4), 8), lax.rem(z + 2 * (m // 4), 8)

    loads = []
    for b in range(BLOCKS):
        loads.append(pltpu.make_async_copy(tok_hbm.at[:, rows(b, CUT)], tok.at[rows(b, 128)], ld_sem.at[b]))
    for b in range(BLOCKS):
        loads.append(pltpu.make_async_copy(grad_hbm.at[:, rows(b, CUT)], grad.at[rows(b, 128)], ld_sem.at[4 + b]))
    loads.append(pltpu.make_async_copy(gu_hbm.at[0], gu, ld_sem.at[8]))
    loads.append(pltpu.make_async_copy(down_hbm.at[0], down, ld_sem.at[9]))

    barrier = pltpu.get_barrier_semaphore()
    for m in (10, 9, 11, 6, 14, 5, 7, 13, 15, 8, 2, 1, 3, 4, 12):
        pl.semaphore_signal(barrier, 1, device_id=dp_at(*peer(m)), device_id_type=MESH)
    for slot in FAR_FIRST:
        pl.semaphore_signal(barrier, 1, device_id=expert_at(slot), device_id_type=MESH)
    for quad in quads:
        for device in quad:
            pl.semaphore_signal(barrier, 1, device_id=device, device_id_type=MESH)
    for load in loads:
        load.start()

    sub = lax.broadcasted_iota(I32, (128, 128), 0)
    lane = lax.broadcasted_iota(I32, (128, 128), 1)
    eye = sub == lane

    def column(row):
        return jnp.sum(jnp.where(eye, row, 0.0), axis=1, keepdims=True)

    ids = ids_ref[...]
    chip = ((ids >> 1) + (8 - x)) & 7
    place = jnp.where(chip > 4, 16 - 2 * chip, jnp.where(chip == 0, 0, 2 * chip - 1))
    slot_row = (2 * place + ((ids + core) & 1)).astype(F32)
    slot_col = column(slot_row)
    same = slot_row == slot_col
    before_row = jnp.sum(jnp.where(same & (sub < lane), 1.0, 0.0), axis=0, keepdims=True)
    before_col = jnp.sum(jnp.where(same & (lane < sub), 1.0, 0.0), axis=1, keepdims=True)
    at_row = (slot_row * float(MSG) + before_row).astype(I32)
    at_col = (slot_col * float(MSG) + before_col).astype(I32)
    weight = column(wt_ref[...])

    down_rows = lax.broadcasted_iota(I32, (16 * MSG, 128), 0)
    for b in range(BLOCKS):
        spread[:, b * 128:(b + 1) * 128] = jnp.where(down_rows == at_row + CAP * b, 1.0, 0.0).astype(BF16)
    for b in range(BLOCKS):
        loads[b].wait()
    snd_t[...] = dot(spread[...], tok[...]).astype(BF16)

    pl.semaphore_wait(barrier, 36)

    def exchange(slot, src, dst, ss, rs):
        other = mirror(slot)
        return pltpu.make_async_remote_copy(
            src.at[rows(slot, MSG)], dst.at[rows(other, MSG)], ss.at[slot], rs.at[other],
            device_id=expert_at(slot), device_id_type=MESH,
        )

    def arrival(slot, src, dst, ss, rs):
        return pltpu.make_async_remote_copy(
            src.at[rows(slot, MSG)], dst.at[rows(slot, MSG)], ss.at[slot], rs.at[slot],
            device_id=expert_at(slot), device_id_type=MESH,
        )

    tset, gset = (snd_t, rcv_t, t_ss, t_rs), (snd_g, rcv_g, g_ss, g_rs)
    rset, dset = (out_r, ret_r, r_ss, r_rs), (out_d, ret_d, d_ss, d_rs)
    for slot in FAR_FIRST:
        exchange(slot, *tset).start()
    for b in range(BLOCKS):
        loads[4 + b].wait()
    for b in range(BLOCKS):
        grad_b = grad[rows(b, 128), :].astype(F32)
        tok[rows(b, 128), :] = (weight * grad_b).astype(BF16)
    snd_g[...] = dot(spread[...], tok[...]).astype(BF16)
    for slot in FAR_FIRST:
        exchange(slot, *gset).start()
    rcv_t[0:MSG, :] = snd_t[0:MSG, :]
    rcv_g[0:MSG, :] = snd_g[0:MSG, :]

    up = lax.broadcasted_iota(I32, (GROUP, GROUP), 0)
    across = lax.broadcasted_iota(I32, (GROUP, GROUP), 1)
    twelfth = (up * 5462) >> 16
    target = (twelfth & 3) * MSG + (twelfth >> 2) * CAP + (up - twelfth * CAP)
    perm[...] = jnp.where(across == target, 1.0, 0.0).astype(BF16)

    def forward(group, m, buf, ss, rs):
        return pltpu.make_async_remote_copy(
            buf.at[rows(4 * group, MSG)], buf.at[rows(4 * group + m, MSG)],
            ss.at[4 * group + m], rs.at[4 * group + m],
            device_id=quads[group // 2][m - 1], device_id_type=MESH,
        )

    ftset, fgset = (xs, ft_ss, ft_rs), (gs, fg_ss, fg_rs)

    def take(group, kind, fkind):
        buf = fkind[0]
        for slot in range(4 * group, 4 * group + 4):
            if slot:
                arrival(slot, *kind).wait_recv()
        turned = dot(perm[...], kind[1][rows(group, GROUP), :]).astype(BF16)
        for b in range(BLOCKS):
            buf[rows(4 * group, MSG), b * CUT:(b + 1) * CUT] = turned[b * MSG:(b + 1) * MSG, :]
        for m in (3, 2, 1):
            forward(group, m, *fkind).start()

    def give(group, value, kind):
        buf = kind[0]
        stacked = jnp.concatenate([value[:, b * CUT:(b + 1) * CUT] for b in range(BLOCKS)], axis=0)
        buf[rows(group, GROUP), :] = dot(perm[...], stacked).astype(BF16)
        for slot in range(4 * group, 4 * group + 4):
            if slot:
                exchange(slot, *kind).start()

    order = (3, 2, 1, 0)
    for group in order:
        take(group, tset, ftset)
    loads[8].wait()
    loads[9].wait()
    for group in order:
        for m in (1, 2, 3):
            forward(group, m, *ftset).wait_recv()
        pre = dot(xs[rows(group, GROUP), :], gu[...])
        a, u = pre[:, :384], pre[:, 384:]
        s = 1.0 / (1.0 + jnp.exp(-a))
        silu = a * s
        act[rows(group, GROUP), :] = (silu * u).astype(BF16)
        p1[rows(group, GROUP), :] = u * s * (1.0 + a * (1.0 - s))
        p2[rows(group, GROUP), :] = silu
    for b in range(BLOCKS):
        right = lax.broadcasted_iota(I32, (128, 16 * MSG), 1)
        gather[rows(b, 128), :] = jnp.where(right == at_col + CAP * b, 1.0, 0.0).astype(BF16)
    for group in order:
        take(group, gset, fgset)
    for group in order:
        result = dot(act[rows(4 * group, MSG), :], down[...]).astype(BF16)
        give(group, result, rset)
    for group in order:
        for m in (1, 2, 3):
            forward(group, m, *fgset).wait_recv()
        d_act = dot(gs[rows(group, GROUP), :], down[...], NT)
        dpre[rows(group, GROUP), 0:384] = (d_act * p1[rows(group, GROUP), :]).astype(BF16)
        dpre[rows(group, GROUP), 384:768] = (d_act * p2[rows(group, GROUP), :]).astype(BF16)

    def share(m):
        yy, zz = peer(m)
        other = ((4 - m // 4) % 4) * 4 + (4 - m % 4) % 4
        return pltpu.make_async_remote_copy(
            part.at[m // 4, yy], got.at[other], w_ss.at[m], w_rs.at[other],
            device_id=dp_at(yy, zz), device_id_type=MESH,
        )

    def shared(m):
        return pltpu.make_async_remote_copy(
            part.at[m // 4, y], got.at[m], w_ss.at[m], w_rs.at[m],
            device_id=dp_at(*peer(m)), device_id_type=MESH,
        )

    for i in (2, 1, 3, 0):
        tile = pl.ds(pl.multiple_of(lax.rem(z + 2 * i, 8) * 128, 128), 128)
        first = dot(xs[:, tile], dpre[...], TN)
        last = dot(gs[:, tile], act[...], TN)
        for j in range(8):
            part[i, j, :, 0:768] = first[j * 16:(j + 1) * 16, :].astype(BF16)
            part[i, j, :, 768:1152] = last[j * 16:(j + 1) * 16, :].astype(BF16)
            if i == 0:
                own[j, :, 0:768] = first[j * 16:(j + 1) * 16, :]
                own[j, :, 768:1152] = last[j * 16:(j + 1) * 16, :]
        for j in (2, 1, 3, 0):
            if i or j:
                share(4 * i + j).start()

    for group in order:
        dx = dot(dpre[rows(4 * group, MSG), :], gu[...], NT).astype(BF16)
        give(group, dx, dset)
    ret_r[0:MSG, :] = out_r[0:MSG, :]
    ret_d[0:MSG, :] = out_d[0:MSG, :]

    for slot in range(1, 16):
        arrival(slot, *rset).wait_recv()
    inner = jnp.zeros((128, 1), F32)
    for b in range(BLOCKS):
        copy_out = dot(gather[rows(b, 128), :], ret_r[...])
        mixed_ref[:, b * CUT:(b + 1) * CUT] = (weight * copy_out).astype(BF16)
        inner = inner + jnp.sum(grad[rows(b, 128), :].astype(F32) * copy_out, axis=1, keepdims=True)
    rwg_ref[...] = jnp.sum(jnp.where(eye, inner, 0.0), axis=0, keepdims=True)
    for slot in range(1, 16):
        arrival(slot, *dset).wait_recv()
    for b in range(BLOCKS):
        tgrad_ref[:, b * CUT:(b + 1) * CUT] = dot(gather[rows(b, 128), :], ret_d[...]).astype(BF16)

    total = own[y]
    for m in range(1, 16):
        shared(m).wait_recv()
        total = total + got[m].astype(F32)
    wgrad_ref[0] = total

    for slot in range(1, 16):
        for kind in (tset, gset, rset, dset):
            exchange(slot, *kind).wait_send()
        share(slot).wait_send()
    for group in range(4):
        for m in (1, 2, 3):
            for kind in (ftset, fgset):
                forward(group, m, *kind).wait_send()


def on_device(tokens, route_ids, route_weight, w_gate_up, w_down, out_grad):
    count, width = tokens.shape
    hidden = w_down.shape[1]
    dma = pltpu.SemaphoreType.DMA
    vmem = pl.BlockSpec(memory_space=pltpu.VMEM)
    hbm = pl.BlockSpec(memory_space=pl.ANY)
    slots = 16 * MSG
    scratch = [
        pltpu.VMEM((512, CUT), BF16), pltpu.VMEM((512, CUT), BF16),
        pltpu.VMEM((width, 2 * hidden), BF16), pltpu.VMEM((hidden, width), BF16),
        pltpu.VMEM((slots, 512), BF16), pltpu.VMEM((512, slots), BF16), pltpu.VMEM((GROUP, GROUP), BF16),
        *[pltpu.VMEM((slots, CUT), BF16)] * 4,
        pltpu.VMEM((slots, width), BF16), pltpu.VMEM((slots, width), BF16),
        pltpu.VMEM((slots, hidden), F32), pltpu.VMEM((slots, hidden), F32),
        pltpu.VMEM((slots, hidden), BF16), pltpu.VMEM((slots, 2 * hidden), BF16),
        *[pltpu.VMEM((slots, CUT), BF16)] * 4,
        pltpu.VMEM((4, 8, 16, 3 * hidden), BF16), pltpu.VMEM((8, 16, 3 * hidden), F32),
        pltpu.VMEM((16, 16, 3 * hidden), BF16),
        dma((10,)), *[dma((16,))] * 14,
    ]
    mixed, tgrad, rwg, wgrad = pl.pallas_call(
        kernel,
        out_shape=(
            jax.ShapeDtypeStruct((count, width), BF16),
            jax.ShapeDtypeStruct((count, width), BF16),
            jax.ShapeDtypeStruct((1, count), F32),
            jax.ShapeDtypeStruct((1, 16, 3 * hidden), F32),
        ),
        in_specs=[vmem, vmem, hbm, hbm, hbm, hbm],
        out_specs=[vmem] * 4,
        scratch_shapes=scratch,
        compiler_params=pltpu.CompilerParams(
            collective_id=0, has_side_effects=True, vmem_limit_bytes=48 * 2**20
        ),
    )(route_ids.reshape(1, count), route_weight.reshape(1, count), tokens, out_grad, w_gate_up, w_down)
    return mixed, tgrad, rwg.reshape(count, 1), wgrad


def solution(mesh):
    rows_split = P(("dp", "expert"), None)
    return jax.shard_map(
        on_device,
        mesh=mesh,
        in_specs=(rows_split, rows_split, rows_split, P("expert", None, None), P("expert", None, None), rows_split),
        out_specs=(rows_split, rows_split, rows_split, P("expert", "dp", None)),
        check_vma=False,
    )
```

time: 266 us -> 88.1 us (0.33); the launches traced: 263 us -> 87.8 us
  waiting for transfers between devices: 197 us -> 0 us
  Pallas kernels: 0 us -> 78.8 us
  starting transfers between devices: 28 us -> 0 us
  between operations: 14.9 us -> 0.66 us
  matrix products: 10.1 us -> 0 us
  other arithmetic: 5.08 us -> 0 us
    unnamed x2 -> x0, waiting for transfers between devices: 137 us -> none
    pallas_call x0 -> x1, Pallas kernels: none -> 78.8 us  [on_device(): pl.pallas_call(kernel, out_shape=(jax.ShapeDtypeStruct((count, width), BF...]
    all_to_all x4 -> x0, waiting for transfers between devices: 60.6 us -> none  [the longest x1 16.1 us: on_device(): lax.all_to_all(outgoing.reshape(experts, capacity, width), 'expert', spli...]
    all_to_all x4 -> x0, starting transfers between devices: 27.9 us -> none  [the longest x1 17.5 us: on_device(): lax.all_to_all(outgoing.reshape(experts, capacity, width), 'expert', spli...]
    dot_general x10 -> x0, matrix products: 10.1 us -> none  [the longest x4 3.59 us: contract_rows(): lax.dot_general(left, right, (((0,), (0,)), ((), ())), preferred_element_...]
    unnamed x12 -> x16, local copies, waits for them, and re-layouts: 2.38 us -> 8.29 us
    reshape x8 -> x0, local copies, waits for them, and re-layouts: 3.86 us -> none  [the longest x1 0.88 us: on_device(): result.reshape(experts, items, width)]
  transfers between devices with their start and end apart: 5 -> 0, of which waited for: 5 -> 0; matrix products, arithmetic and copies ran while one was open for 4% -> 0% of each run, Pallas kernels for 0% -> 0%
where the time goes in v1:
time: 88.1 us; the launch traced here: 87.8 us
  Pallas kernels  78.8 us (89%)
  local copies, waits for them, and re-layouts  8.29 us (9%)
    pallas_call x1, Pallas kernels, on_device(): pl.pallas_call(kernel, out_shape=(jax.ShapeDtypeStruct((count, width), BF...  78.8 us
    unnamed x16, local copies, waits for them, and re-layouts  8.29 us

profile of v1, /device:TPU:1, one launch (start us, length us, event | category | flops | bytes accessed | tf_op | source)
XLA Modules:
  0.0 87.8 jit_solution(7724712175229551760)
XLA Ops:
  0.6 0.0 copy-start
  0.6 1.4 %copy-done = bf16[1,1024,768]{2,1,0:T(8,128)(2,1)S(1)} copy-done((bf16[1,1024,768]{2,1,0:T(8,128)(2,1)S(1)}, bf16[1,1024,768]{2,1,0:T(8,128)(2,1)}, u32[]{:S(2)}) %copy-start) | copy-done | bytes 1572888
  2.0 0.0 copy-start.1
  2.0 1.1 %copy-done.1 = bf16[1,384,1024]{2,1,0:T(8,128)(2,1)S(1)} copy-done((bf16[1,384,1024]{2,1,0:T(8,128)(2,1)S(1)}, bf16[1,384,1024]{2,1,0:T(8,128)(2,1)}, u32[]{:S(2)}) %copy-start.1) | copy-done | bytes 786456
  3.2 0.0 copy-start.2
  3.2 0.9 %copy-done.2 = bf16[128,1024]{1,0:T(8,128)(2,1)S(1)} copy-done((bf16[128,1024]{1,0:T(8,128)(2,1)S(1)}, bf16[128,1024]{1,0:T(8,128)(2,1)}, u32[]{:S(2)}) %copy-start.2) | copy-done | bytes 262168
  4.1 0.0 copy-start.3
  4.1 0.9 %copy-done.3 = bf16[128,1024]{1,0:T(8,128)(2,1)S(1)} copy-done((bf16[128,1024]{1,0:T(8,128)(2,1)S(1)}, bf16[128,1024]{1,0:T(8,128)(2,1)}, u32[]{:S(2)}) %copy-start.3) | copy-done | bytes 262168
  5.1 0.0 copy-start.4
  5.1 0.7 copy-done.4
  5.7 0.0 copy-start.5
  5.7 0.7 copy-done.5
  6.4 78.8 %shard_map.93 = (bf16[128,1024]{1,0:T(8,128)(2,1)S(1)}, bf16[128,1024]{1,0:T(8,128)(2,1)S(1)}, f32[1,128]{1,0:T(1,128)S(1)}, f32[1,16,1152]{2,1,0:T(8,128)S(1)}) custom-call(s32[1,128]{1,0:T(1,128)S(1)} %bitcast.3, f32[1,128]{1,0:T(1,128)S(1)} %bitcast.4, bf16[128,1024]{1,0:T(8,128)(2,1)S(1)} %copy-done.2, bf16[128,1024]{1,0:T(8,128)(2,1)S(1)} %copy-done.3, ...), custom_call_target="tpu_custom_call" | custom-call | tf_op jit(solution)/shard_map/pallas_call | solution.py:288
  85.2 0.7 copy.14
  85.9 0.7 copy.15
  86.7 0.5 copy.16
  87.2 0.6 copy.17
Async XLA Ops:
  0.6 1.4 %copy-start = (bf16[1,1024,768]{2,1,0:T(8,128)(2,1)S(1)}, bf16[1,1024,768]{2,1,0:T(8,128)(2,1)}, u32[]{:S(2)}) copy-start(bf16[1,1024,768]{2,1,0:T(8,128)(2,1)} %gu_hbm.1) | copy-start | bytes 4718596
  2.0 1.1 %copy-start.1 = (bf16[1,384,1024]{2,1,0:T(8,128)(2,1)S(1)}, bf16[1,384,1024]{2,1,0:T(8,128)(2,1)}, u32[]{:S(2)}) copy-start(bf16[1,384,1024]{2,1,0:T(8,128)(2,1)} %down_hbm.1) | copy-start | bytes 2359300
  3.2 0.9 %copy-start.2 = (bf16[128,1024]{1,0:T(8,128)(2,1)S(1)}, bf16[128,1024]{1,0:T(8,128)(2,1)}, u32[]{:S(2)}) copy-start(bf16[128,1024]{1,0:T(8,128)(2,1)} %tok_hbm.1) | copy-start | bytes 786436
  4.1 0.9 %copy-start.3 = (bf16[128,1024]{1,0:T(8,128)(2,1)S(1)}, bf16[128,1024]{1,0:T(8,128)(2,1)}, u32[]{:S(2)}) copy-start(bf16[128,1024]{1,0:T(8,128)(2,1)} %grad_hbm.1) | copy-start | bytes 786436
  5.1 0.7 copy-start.4
  5.7 0.7 copy-start.5

commit v2 on v1

v2 whole, which is shorter than its diff:
```python
import jax
import jax.numpy as jnp
from jax import lax
from jax.experimental import pallas as pl
from jax.experimental.pallas import tpu as pltpu
from jax.sharding import PartitionSpec as P

MESH = pl.DeviceIdType.MESH
BF16, F32, I32 = jnp.bfloat16, jnp.float32, jnp.int32
CAP = 12
BLOCKS = 4
CUT = 256
MSG = CAP * BLOCKS
GROUP = 4 * MSG
CHIPS = (0, 1, 7, 2, 6, 3, 5, 4)
PLACE = {k: i for i, k in enumerate(CHIPS)}
FAR_FIRST = (14, 15, 12, 13, 10, 11, 8, 9, 6, 7, 4, 5, 2, 3, 1)
ORDER = (3, 2, 1, 0)
PEERS = (10, 9, 11, 6, 14, 5, 7, 13, 15, 8, 2, 1, 3, 4, 12)
HALF = 2 * MSG
NT = (((1,), (1,)), ((), ()))
TN = (((0,), (0,)), ((), ()))


def mirror(slot):
    return 2 * PLACE[(8 - CHIPS[slot // 2]) % 8] + slot % 2


def rows(at, n):
    return pl.ds(at * n, n)


def dot(a, b, dims=(((1,), (0,)), ((), ()))):
    return lax.dot_general(a, b, dims, preferred_element_type=F32)


def kernel(
    ids_hbm, wt_hbm, tok_hbm, grad_hbm, gu_hbm, down_hbm,
    mixed_ref, tgrad_ref, rwg_ref, wgrad_ref,
    ids_ref, wt_ref, tok, grad, gu, down, spread, gather, perm, picks,
    snd_t, snd_g, rcv_t, rcv_g, xs, gs, p1, p2, e_snd, e_all, l_snd, l_all,
    out_r, out_d, ret_r, ret_d, part, own, got,
    ld_sem, t_ss, t_rs, g_ss, g_rs, r_ss, r_rs, d_ss, d_rs,
    e_ss, e_rs, l_ss, l_rs, w_ss, w_rs,
):
    dp, ex = lax.axis_index("dp"), lax.axis_index("expert")
    y, z = lax.rem(dp, 8), lax.div(dp, 8)
    x, core = lax.div(ex, 2), lax.rem(ex, 2)

    def expert_at(slot):
        chip = lax.rem(x + CHIPS[slot // 2], 8)
        return {"expert": chip * 2 + (core if slot % 2 == 0 else 1 - core)}

    def dp_at(yy, zz):
        return {"dp": zz * 8 + yy}

    y0, z0 = y + 1 - 2 * lax.rem(y, 2), z + 1 - 2 * lax.rem(z, 2)
    y1, z1 = lax.rem(y + 7 + 2 * lax.rem(y, 2), 8), lax.rem(z + 7 + 2 * lax.rem(z, 2), 8)
    quads = (
        (dp_at(y0, z), dp_at(y, z0), dp_at(y0, z0)),
        (dp_at(y1, z), dp_at(y, z1), dp_at(y1, z1)),
    )

    def peer(m):
        return lax.rem(y + 2 * (m % 4), 8), lax.rem(z + 2 * (m // 4), 8)

    loads = [
        pltpu.make_async_copy(ids_hbm, ids_ref, ld_sem.at[10]),
        pltpu.make_async_copy(wt_hbm, wt_ref, ld_sem.at[11]),
    ]
    for b in range(BLOCKS):
        loads.append(pltpu.make_async_copy(tok_hbm.at[:, rows(b, CUT)], tok.at[rows(b, 128)], ld_sem.at[b]))
    for b in range(BLOCKS):
        loads.append(pltpu.make_async_copy(grad_hbm.at[:, rows(b, CUT)], grad.at[rows(b, 128)], ld_sem.at[4 + b]))
    loads.append(pltpu.make_async_copy(gu_hbm.at[0], gu, ld_sem.at[8]))
    loads.append(pltpu.make_async_copy(down_hbm.at[0], down, ld_sem.at[9]))

    barrier = pltpu.get_barrier_semaphore()
    for load in loads[:2]:
        load.start()
    for slot in FAR_FIRST:
        pl.semaphore_signal(barrier, 1, device_id=expert_at(slot), device_id_type=MESH)
    for load in loads[2:]:
        load.start()
    for m in PEERS:
        pl.semaphore_signal(barrier, 1, device_id=dp_at(*peer(m)), device_id_type=MESH)
    for quad in quads:
        for device in quad:
            pl.semaphore_signal(barrier, 1, device_id=device, device_id_type=MESH)

    sub = lax.broadcasted_iota(I32, (128, 128), 0)
    lane = lax.broadcasted_iota(I32, (128, 128), 1)
    eye = sub == lane

    def column(row):
        return jnp.sum(jnp.where(eye, row, 0.0), axis=1, keepdims=True)

    loads[0].wait()
    loads[1].wait()
    ids = ids_ref[...]
    chip = ((ids >> 1) + (8 - x)) & 7
    place = jnp.where(chip > 4, 16 - 2 * chip, jnp.where(chip == 0, 0, 2 * chip - 1))
    slot_row = (2 * place + ((ids + core) & 1)).astype(F32)
    slot_col = column(slot_row)
    same = slot_row == slot_col
    before_row = jnp.sum(jnp.where(same & (sub < lane), 1.0, 0.0), axis=0, keepdims=True)
    before_col = jnp.sum(jnp.where(same & (lane < sub), 1.0, 0.0), axis=1, keepdims=True)
    at_row = (slot_row * float(MSG) + before_row).astype(I32)
    at_col = (slot_col * float(MSG) + before_col).astype(I32)
    weight = column(wt_ref[...])

    down_rows = lax.broadcasted_iota(I32, (16 * MSG, 128), 0)
    for b in range(BLOCKS):
        spread[:, b * 128:(b + 1) * 128] = jnp.where(down_rows == at_row + CAP * b, 1.0, 0.0).astype(BF16)
    for b in range(BLOCKS):
        loads[2 + b].wait()
    snd_t[...] = dot(spread[...], tok[...]).astype(BF16)

    pl.semaphore_wait(barrier, 36)

    def exchange(slot, src, dst, ss, rs):
        other = mirror(slot)
        return pltpu.make_async_remote_copy(
            src.at[rows(slot, MSG)], dst.at[rows(other, MSG)], ss.at[slot], rs.at[other],
            device_id=expert_at(slot), device_id_type=MESH,
        )

    def arrival(slot, src, dst, ss, rs):
        return pltpu.make_async_remote_copy(
            src.at[rows(slot, MSG)], dst.at[rows(slot, MSG)], ss.at[slot], rs.at[slot],
            device_id=expert_at(slot), device_id_type=MESH,
        )

    tset, gset = (snd_t, rcv_t, t_ss, t_rs), (snd_g, rcv_g, g_ss, g_rs)
    rset, dset = (out_r, ret_r, r_ss, r_rs), (out_d, ret_d, d_ss, d_rs)
    for slot in FAR_FIRST:
        exchange(slot, *tset).start()
    for b in range(BLOCKS):
        loads[6 + b].wait()
    for b in range(BLOCKS):
        grad_b = grad[rows(b, 128), :].astype(F32)
        tok[rows(b, 128), :] = (weight * grad_b).astype(BF16)
    snd_g[...] = dot(spread[...], tok[...]).astype(BF16)
    for slot in FAR_FIRST:
        exchange(slot, *gset).start()
    rcv_t[0:MSG, :] = snd_t[0:MSG, :]
    rcv_g[0:MSG, :] = snd_g[0:MSG, :]

    up = lax.broadcasted_iota(I32, (GROUP, GROUP), 0)
    across = lax.broadcasted_iota(I32, (GROUP, GROUP), 1)
    twelfth = (up * 5462) >> 16
    target = (twelfth & 3) * MSG + (twelfth >> 2) * CAP + (up - twelfth * CAP)
    perm[...] = jnp.where(across == target, 1.0, 0.0).astype(BF16)
    for b in range(BLOCKS):
        right = lax.broadcasted_iota(I32, (128, 16 * MSG), 1)
        gather[rows(b, 128), :] = jnp.where(right == at_col + CAP * b, 1.0, 0.0).astype(BF16)

    lanes_in = lax.broadcasted_iota(I32, (256, 128), 0)
    lanes_out = lax.broadcasted_iota(I32, (256, 128), 1)
    goal = (lanes_in >> 7) * 64 + ((lanes_in >> 5) & 3) * 16 + (lanes_in & 15)
    odd_y, odd_z = lax.rem(y, 2), lax.rem(z, 2)
    for flip in range(2):
        parity = odd_y if flip == 0 else 1 - odd_y
        picks[flip] = jnp.where((lanes_out == goal) & (((lanes_in >> 4) & 1) == parity), 1.0, 0.0).astype(BF16)

    def pack(buf, at):
        classes = [None] * 4
        for flip in range(2):
            pieces = []
            for odd in (odd_z, 1 - odd_z):
                for h in range(2):
                    left = pl.ds(pl.multiple_of((odd + 4 * h) * 128, 128), 128)
                    right = pl.ds(pl.multiple_of((odd + 4 * h + 2) * 128, 128), 128)
                    pieces.append(jnp.concatenate([buf[at, left], buf[at, right]], axis=1))
            chosen = dot(jnp.concatenate(pieces, axis=0), picks[flip]).astype(BF16)
            for k in range(2):
                classes[flip + 2 * k] = (
                    chosen[2 * k * HALF:(2 * k + 1) * HALF, :], chosen[(2 * k + 1) * HALF:(2 * k + 2) * HALF, :]
                )
        return classes

    def forward(group, m, src, dst, ss, rs):
        return pltpu.make_async_remote_copy(
            src.at[rows(4 * (m - 1) + group, MSG)], dst.at[rows(4 * m + group, MSG)],
            ss.at[4 * m + group], rs.at[4 * m + group],
            device_id=quads[group % 2][m - 1], device_id_type=MESH,
        )

    eset, lset = (e_snd, e_all, e_ss, e_rs), (l_snd, l_all, l_ss, l_rs)

    def take(group, kind, buf):
        for slot in range(4 * group + 3, 4 * group - 1, -1):
            if slot:
                arrival(slot, *kind).wait_recv()
        turned = dot(perm[...], kind[1][rows(group, GROUP), :]).astype(BF16)
        for b in range(BLOCKS):
            buf[rows(group, MSG), b * CUT:(b + 1) * CUT] = turned[b * MSG:(b + 1) * MSG, :]

    def spill(half, classes, width, values, kind):
        at = rows(half, HALF)
        for m in (3, 2, 1, 0):
            buf = kind[0] if m else kind[1]
            place = pl.ds((GROUP * (m - 1) if m else 0) + half * HALF, HALF)
            buf[place, 0:128] = classes[m][0]
            buf[place, 128:256] = classes[m][1]
            for i, value in enumerate(values):
                buf[place, 256 + i * width:256 + (i + 1) * width] = value
            if m:
                for group in (2 * half + 1, 2 * half):
                    forward(group, m, *kind).start()

    def early(half):
        at = rows(half, HALF)
        pre = dot(xs[at, :], gu[...])
        a, u = pre[:, :384], pre[:, 384:]
        s = 1.0 / (1.0 + jnp.exp(-a))
        silu = a * s
        p1[at, :] = u * s * (1.0 + a * (1.0 - s))
        p2[at, :] = silu
        spill(half, pack(xs, at), 384, [(silu * u).astype(BF16)], eset)

    def late(half):
        at = rows(half, HALF)
        d_act = dot(gs[at, :], down[...], NT)
        spill(half, pack(gs, at), 384, [(d_act * p1[at, :]).astype(BF16), (d_act * p2[at, :]).astype(BF16)], lset)

    def give(value, kind):
        buf = kind[0]
        for group in ORDER:
            stacked = jnp.concatenate(
                [value[group * MSG:(group + 1) * MSG, b * CUT:(b + 1) * CUT] for b in range(BLOCKS)], axis=0
            )
            buf[rows(group, GROUP), :] = dot(perm[...], stacked).astype(BF16)
            for slot in range(4 * group + 3, 4 * group - 1, -1):
                if slot:
                    exchange(slot, *kind).start()

    take(3, tset, xs)
    take(2, tset, xs)
    loads[10].wait()
    loads[11].wait()
    early(1)
    take(1, tset, xs)
    take(0, tset, xs)
    early(0)
    give(dot(e_all[rows(0, GROUP), 256:640], down[...]).astype(BF16), rset)
    take(3, gset, gs)
    take(2, gset, gs)
    late(1)
    take(1, gset, gs)
    take(0, gset, gs)
    late(0)
    give(dot(l_all[rows(0, GROUP), 256:1024], gu[...], NT).astype(BF16), dset)

    def share(m):
        yy, zz = peer(m)
        other = ((4 - m // 4) % 4) * 4 + (4 - m % 4) % 4
        return pltpu.make_async_remote_copy(
            part.at[lax.div(zz, 2) * 4 + lax.div(yy, 2)], got.at[other], w_ss.at[m], w_rs.at[other],
            device_id=dp_at(yy, zz), device_id_type=MESH,
        )

    def shared(m):
        return pltpu.make_async_remote_copy(
            part.at[m], got.at[m], w_ss.at[m], w_rs.at[m],
            device_id=dp_at(*peer(m)), device_id_type=MESH,
        )

    for m in (1, 2, 3):
        for group in ORDER:
            forward(group, m, *eset).wait_recv()
            forward(group, m, *lset).wait_recv()
    first = dot(e_all[:, 0:256], l_all[:, 256:1024], TN)
    last = dot(l_all[:, 0:256], e_all[:, 256:640], TN)
    for k in range(16):
        part[k, :, 0:768] = first[k * 16:(k + 1) * 16, :].astype(BF16)
        part[k, :, 768:1152] = last[k * 16:(k + 1) * 16, :].astype(BF16)
    for m in PEERS:
        share(m).start()
    for k in range(16):
        own[k, :, 0:768] = first[k * 16:(k + 1) * 16, :]
        own[k, :, 768:1152] = last[k * 16:(k + 1) * 16, :]

    ret_r[0:MSG, :] = out_r[0:MSG, :]
    ret_d[0:MSG, :] = out_d[0:MSG, :]
    for slot in range(1, 16):
        arrival(slot, *rset).wait_recv()
    inner = jnp.zeros((128, 1), F32)
    for b in range(BLOCKS):
        copy_out = dot(gather[rows(b, 128), :], ret_r[...])
        mixed_ref[:, b * CUT:(b + 1) * CUT] = (weight * copy_out).astype(BF16)
        inner = inner + jnp.sum(grad[rows(b, 128), :].astype(F32) * copy_out, axis=1, keepdims=True)
    rwg_ref[...] = jnp.sum(jnp.where(eye, inner, 0.0), axis=0, keepdims=True)
    for slot in range(1, 16):
        arrival(slot, *dset).wait_recv()
    for b in range(BLOCKS):
        tgrad_ref[:, b * CUT:(b + 1) * CUT] = dot(gather[rows(b, 128), :], ret_d[...]).astype(BF16)

    total = own[lax.div(z, 2) * 4 + lax.div(y, 2)]
    for m in range(1, 16):
        shared(m).wait_recv()
        total = total + got[m].astype(F32)
    wgrad_ref[0] = total

    for slot in range(1, 16):
        for kind in (tset, gset, rset, dset):
            exchange(slot, *kind).wait_send()
        share(slot).wait_send()
    for group in range(4):
        for m in (1, 2, 3):
            for kind in (eset, lset):
                forward(group, m, *kind).wait_send()


def hand_over(*refs):
    taken, given, sem = refs[:4], refs[4:8], refs[8]
    copies = [pltpu.make_async_copy(a, b, sem.at[i]) for i, (a, b) in enumerate(zip(taken, given))]
    for copy in copies:
        copy.start()
    for copy in copies:
        copy.wait()


def on_device(tokens, route_ids, route_weight, w_gate_up, w_down, out_grad):
    count, width = tokens.shape
    hidden = w_down.shape[1]
    dma = pltpu.SemaphoreType.DMA
    vmem = pl.BlockSpec(memory_space=pltpu.VMEM)
    hbm = pl.BlockSpec(memory_space=pl.ANY)
    slots = 16 * MSG
    scratch = [
        pltpu.VMEM((1, count), I32), pltpu.VMEM((1, count), F32),
        pltpu.VMEM((512, CUT), BF16), pltpu.VMEM((512, CUT), BF16),
        pltpu.VMEM((width, 2 * hidden), BF16), pltpu.VMEM((hidden, width), BF16),
        pltpu.VMEM((slots, 512), BF16), pltpu.VMEM((512, slots), BF16), pltpu.VMEM((GROUP, GROUP), BF16),
        pltpu.VMEM((2, 256, 128), BF16),
        *[pltpu.VMEM((slots, CUT), BF16)] * 4,
        pltpu.VMEM((GROUP, width), BF16), pltpu.VMEM((GROUP, width), BF16),
        pltpu.VMEM((GROUP, hidden), F32), pltpu.VMEM((GROUP, hidden), F32),
        pltpu.VMEM((3 * GROUP, 256 + hidden), BF16), pltpu.VMEM((4 * GROUP, 256 + hidden), BF16),
        pltpu.VMEM((3 * GROUP, 256 + 2 * hidden), BF16), pltpu.VMEM((4 * GROUP, 256 + 2 * hidden), BF16),
        *[pltpu.VMEM((slots, CUT), BF16)] * 4,
        pltpu.VMEM((16, 16, 3 * hidden), BF16), pltpu.VMEM((16, 16, 3 * hidden), F32),
        pltpu.VMEM((16, 16, 3 * hidden), BF16),
        dma((12,)), *[dma((16,))] * 14,
    ]
    outs = (
        jax.ShapeDtypeStruct((count, width), BF16),
        jax.ShapeDtypeStruct((count, width), BF16),
        jax.ShapeDtypeStruct((1, count), F32),
        jax.ShapeDtypeStruct((1, 16, 3 * hidden), F32),
    )
    made = pl.pallas_call(
        kernel,
        out_shape=outs,
        in_specs=[hbm] * 6,
        out_specs=[vmem] * 4,
        scratch_shapes=scratch,
        compiler_params=pltpu.CompilerParams(
            collective_id=0, has_side_effects=True, vmem_limit_bytes=58 * 2**20
        ),
    )(route_ids.reshape(1, count), route_weight.reshape(1, count), tokens, out_grad, w_gate_up, w_down)
    mixed, tgrad, rwg, wgrad = pl.pallas_call(
        hand_over,
        out_shape=outs,
        in_specs=[vmem] * 4,
        out_specs=[hbm] * 4,
        scratch_shapes=[dma((4,))],
    )(*made)
    return mixed, tgrad, rwg.reshape(count, 1), wgrad


def solution(mesh):
    rows_split = P(("dp", "expert"), None)
    return jax.shard_map(
        on_device,
        mesh=mesh,
        in_specs=(rows_split, rows_split, rows_split, P("expert", None, None), P("expert", None, None), rows_split),
        out_specs=(rows_split, rows_split, rows_split, P("expert", "dp", None)),
        check_vma=False,
    )
```

time: 88.1 us -> 76.9 us (0.87)
  local copies, waits for them, and re-layouts: 8.29 us -> 0 us
  Pallas kernels: 78.8 us -> 75.6 us
    unnamed x16 -> x0, local copies, waits for them, and re-layouts: 8.29 us -> none
    pallas_call x1 -> x2, Pallas kernels: 78.8 us -> 75.6 us  [the longest x1 73.7 us: on_device(): pl.pallas_call(kernel, out_shape=outs, in_specs=[hbm] * 6, out_specs=[vme...]
where the time goes in v2:
time: 76.9 us; the launch traced here: 76.3 us
  Pallas kernels  75.6 us (98%)
    pallas_call x1, Pallas kernels, on_device(): pl.pallas_call(kernel, out_shape=outs, in_specs=[hbm] * 6, out_specs=[vme...  73.7 us
    pallas_call x1, Pallas kernels, on_device(): pl.pallas_call(hand_over, out_shape=outs, in_specs=[vmem] * 4, out_specs=...  1.89 us

profile of v2, /device:TPU:1, one launch (start us, length us, event | category | flops | bytes accessed | tf_op | source)
XLA Modules:
  0.0 76.3 jit_solution(15246330584827226258)
XLA Ops:
  0.6 73.7 %shard_map.93 = (bf16[128,1024]{1,0:T(8,128)(2,1)}, bf16[128,1024]{1,0:T(8,128)(2,1)}, f32[1,128]{1,0:T(1,128)}, f32[1,16,1152]{2,1,0:T(8,128)}) custom-call(s32[1,128]{1,0:T(1,128)} %bitcast.3, f32[1,128]{1,0:T(1,128)} %bitcast.4, bf16[128,1024]{1,0:T(8,128)(2,1)} %tok_hbm.1, bf16[128,1024]{1,0:T(8,128)(2,1)} %grad_hbm.1, bf16[1,1024,768]{2,1,0:T(8,128)(2,1)} %gu_hbm.1, ...), custom_call_target="tpu_custom_call" | custom-call | tf_op jit(solution)/shard_map/pallas_call | solution.py:353
  74.4 1.9 %shard_map.94 = (bf16[128,1024]{1,0:T(8,128)(2,1)}, bf16[128,1024]{1,0:T(8,128)(2,1)}, f32[1,128]{1,0:T(1,128)}, f32[1,16,1152]{2,1,0:T(8,128)}) custom-call(bf16[128,1024]{1,0:T(8,128)(2,1)} %get-tuple-element.12.refs_0_, bf16[128,1024]{1,0:T(8,128)(2,1)} %get-tuple-element.13.refs_1_, f32[1,128]{1,0:T(1,128)} %get-tuple-element.14.refs_2_, ...), custom_call_target="tpu_custom_call" | custom-call | tf_op jit(solution)/shard_map/pallas_call | solution.py:363

commit v3 on v2

--- a/solution.py
+++ b/solution.py
@@ -41,7 +41,7 @@
     snd_t, snd_g, rcv_t, rcv_g, xs, gs, p1, p2, e_snd, e_all, l_snd, l_all,
     out_r, out_d, ret_r, ret_d, part, own, got,
     ld_sem, t_ss, t_rs, g_ss, g_rs, r_ss, r_rs, d_ss, d_rs,
-    e_ss, e_rs, l_ss, l_rs, w_ss, w_rs,
+    e_ss, e_rs, l_ss, l_rs, w_ss, w_rs, here,
 ):
     dp, ex = lax.axis_index("dp"), lax.axis_index("expert")
     y, z = lax.rem(dp, 8), lax.div(dp, 8)
@@ -80,13 +80,13 @@
         load.start()
     for slot in FAR_FIRST:
         pl.semaphore_signal(barrier, 1, device_id=expert_at(slot), device_id_type=MESH)
-    for load in loads[2:]:
-        load.start()
-    for m in PEERS:
+    for m in (2, 1, 3):
         pl.semaphore_signal(barrier, 1, device_id=dp_at(*peer(m)), device_id_type=MESH)
     for quad in quads:
         for device in quad:
             pl.semaphore_signal(barrier, 1, device_id=device, device_id_type=MESH)
+    for load in loads[2:]:
+        load.start()
 
     sub = lax.broadcasted_iota(I32, (128, 128), 0)
     lane = lax.broadcasted_iota(I32, (128, 128), 1)
@@ -116,7 +116,7 @@
         loads[2 + b].wait()
     snd_t[...] = dot(spread[...], tok[...]).astype(BF16)
 
-    pl.semaphore_wait(barrier, 36)
+    pl.semaphore_wait(barrier, 24)
 
     def exchange(slot, src, dst, ss, rs):
         other = mirror(slot)
@@ -143,6 +143,12 @@
     snd_g[...] = dot(spread[...], tok[...]).astype(BF16)
     for slot in FAR_FIRST:
         exchange(slot, *gset).start()
+
+    def tell(i, zz):
+        pl.semaphore_signal(here.at[i], 1, device_id=dp_at(y, zz), device_id_type=MESH)
+
+    tell(0, z0)
+    tell(1, z1)
     rcv_t[0:MSG, :] = snd_t[0:MSG, :]
     rcv_g[0:MSG, :] = snd_g[0:MSG, :]
 
@@ -179,9 +185,12 @@
                 )
         return classes
 
+    def spot(m, group):
+        return (group // 2) * 8 + 2 * m + group % 2
+
     def forward(group, m, src, dst, ss, rs):
         return pltpu.make_async_remote_copy(
-            src.at[rows(4 * (m - 1) + group, MSG)], dst.at[rows(4 * m + group, MSG)],
+            src.at[rows(4 * (m - 1) + group, MSG)], dst.at[rows(spot(m, group), MSG)],
             ss.at[4 * m + group], rs.at[4 * m + group],
             device_id=quads[group % 2][m - 1], device_id_type=MESH,
         )
@@ -197,10 +206,9 @@
             buf[rows(group, MSG), b * CUT:(b + 1) * CUT] = turned[b * MSG:(b + 1) * MSG, :]
 
     def spill(half, classes, width, values, kind):
-        at = rows(half, HALF)
         for m in (3, 2, 1, 0):
             buf = kind[0] if m else kind[1]
-            place = pl.ds((GROUP * (m - 1) if m else 0) + half * HALF, HALF)
+            place = pl.ds(GROUP * (m - 1) + half * HALF if m else 4 * half * HALF, HALF)
             buf[place, 0:128] = classes[m][0]
             buf[place, 128:256] = classes[m][1]
             for i, value in enumerate(values):
@@ -235,6 +243,9 @@
                 if slot:
                     exchange(slot, *kind).start()
 
+    def mine(buf, low, high):
+        return jnp.concatenate([buf[rows(4 * half, HALF), low:high] for half in range(2)], axis=0)
+
     take(3, tset, xs)
     take(2, tset, xs)
     loads[10].wait()
@@ -243,14 +254,21 @@
     take(1, tset, xs)
     take(0, tset, xs)
     early(0)
-    give(dot(e_all[rows(0, GROUP), 256:640], down[...]).astype(BF16), rset)
+    give(dot(mine(e_all, 256, 640), down[...]).astype(BF16), rset)
+    pl.semaphore_wait(here.at[0], 1)
+    pl.semaphore_wait(here.at[1], 1)
+    tell(2, lax.rem(z + 2, 8))
+    tell(3, lax.rem(z + 6, 8))
     take(3, gset, gs)
     take(2, gset, gs)
     late(1)
+    pl.semaphore_wait(here.at[2], 1)
+    pl.semaphore_wait(here.at[3], 1)
+    tell(4, lax.rem(z + 4, 8))
     take(1, gset, gs)
     take(0, gset, gs)
     late(0)
-    give(dot(l_all[rows(0, GROUP), 256:1024], gu[...], NT).astype(BF16), dset)
+    give(dot(mine(l_all, 256, 1024), gu[...], NT).astype(BF16), dset)
 
     def share(m):
         yy, zz = peer(m)
@@ -266,12 +284,16 @@
             device_id=dp_at(*peer(m)), device_id_type=MESH,
         )
 
-    for m in (1, 2, 3):
-        for group in ORDER:
-            forward(group, m, *eset).wait_recv()
-            forward(group, m, *lset).wait_recv()
-    first = dot(e_all[:, 0:256], l_all[:, 256:1024], TN)
-    last = dot(l_all[:, 0:256], e_all[:, 256:640], TN)
+    first = last = 0.0
+    for half in (1, 0):
+        for m in (1, 2, 3):
+            for group in (2 * half + 1, 2 * half):
+                forward(group, m, *eset).wait_recv()
+                forward(group, m, *lset).wait_recv()
+        at = rows(half, 4 * HALF)
+        first = first + dot(e_all[at, 0:256], l_all[at, 256:1024], TN)
+        last = last + dot(l_all[at, 0:256], e_all[at, 256:640], TN)
+    pl.semaphore_wait(here.at[4], 1)
     for k in range(16):
         part[k, :, 0:768] = first[k * 16:(k + 1) * 16, :].astype(BF16)
         part[k, :, 768:1152] = last[k * 16:(k + 1) * 16, :].astype(BF16)
@@ -343,6 +365,7 @@
         pltpu.VMEM((16, 16, 3 * hidden), BF16), pltpu.VMEM((16, 16, 3 * hidden), F32),
         pltpu.VMEM((16, 16, 3 * hidden), BF16),
         dma((12,)), *[dma((16,))] * 14,
+        pltpu.SemaphoreType.REGULAR((5,)),
     ]
     outs = (
         jax.ShapeDtypeStruct((count, width), BF16),
@@ -352,7 +375,7 @@
     )
     made = pl.pallas_call(
         kernel,
-        out_shape=outs,
+        out_shape=tuple(pltpu.VMEM(o.shape, o.dtype) for o in outs),
         in_specs=[hbm] * 6,
         out_specs=[vmem] * 4,
         scratch_shapes=scratch,
@@ -366,6 +389,7 @@
         in_specs=[vmem] * 4,
         out_specs=[hbm] * 4,
         scratch_shapes=[dma((4,))],
+        compiler_params=pltpu.CompilerParams(vmem_limit_bytes=2**21),
     )(*made)
     return mixed, tgrad, rwg.reshape(count, 1), wgrad
 

time: 76.9 us -> 73.4 us (0.954)
  Pallas kernels: 75.6 us -> 72.6 us
    pallas_call x1, Pallas kernels: 73.7 us -> 71.8 us  [on_device(): pl.pallas_call(kernel, out_shape=tuple((pltpu.VMEM(o.shape, o.dtype) for...]
    pallas_call x1, Pallas kernels: 1.89 us -> 0.85 us  [on_device(): pl.pallas_call(hand_over, out_shape=outs, in_specs=[vmem] * 4, out_specs=...]
where the time goes in v3:
time: 73.4 us; the launch traced here: 73.3 us
  Pallas kernels  72.6 us (99%)
    pallas_call x1, Pallas kernels, on_device(): pl.pallas_call(kernel, out_shape=tuple((pltpu.VMEM(o.shape, o.dtype) for...  71.8 us

profile of v3, /device:TPU:1, one launch (start us, length us, event | category | flops | bytes accessed | tf_op | source)
XLA Modules:
  0.0 73.3 jit_solution(1851419266825326222)
XLA Ops:
  0.6 71.8 %shard_map.93 = (bf16[128,1024]{1,0:T(8,128)(2,1)S(1)}, bf16[128,1024]{1,0:T(8,128)(2,1)S(1)}, f32[1,128]{1,0:T(1,128)S(1)}, f32[1,16,1152]{2,1,0:T(8,128)S(1)}) custom-call(s32[1,128]{1,0:T(1,128)} %bitcast.3, f32[1,128]{1,0:T(1,128)} %bitcast.4, bf16[128,1024]{1,0:T(8,128)(2,1)} %tok_hbm.1, bf16[128,1024]{1,0:T(8,128)(2,1)} %grad_hbm.1, ...), custom_call_target="tpu_custom_call" | custom-call | tf_op jit(solution)/shard_map/pallas_call | solution.py:376
  72.4 0.8 %shard_map.94 = (bf16[128,1024]{1,0:T(8,128)(2,1)}, bf16[128,1024]{1,0:T(8,128)(2,1)}, f32[1,128]{1,0:T(1,128)}, f32[1,16,1152]{2,1,0:T(8,128)}) custom-call(bf16[128,1024]{1,0:T(8,128)(2,1)S(1)} %get-tuple-element.12.refs_0_, bf16[128,1024]{1,0:T(8,128)(2,1)S(1)} %get-tuple-element.13.refs_1_, f32[1,128]{1,0:T(1,128)S(1)} %get-tuple-element.14.refs_2_, ...), custom_call_target="tpu_custom_call" | custom-call | tf_op jit(solution)/shard_map/pallas_call | solution.py:386

commit v4 on v3

--- a/solution.py
+++ b/solution.py
@@ -38,10 +38,10 @@
     ids_hbm, wt_hbm, tok_hbm, grad_hbm, gu_hbm, down_hbm,
     mixed_ref, tgrad_ref, rwg_ref, wgrad_ref,
     ids_ref, wt_ref, tok, grad, gu, down, spread, gather, perm, picks,
-    snd_t, snd_g, rcv_t, rcv_g, xs, gs, p1, p2, e_snd, e_all, l_snd, l_all,
-    out_r, out_d, ret_r, ret_d, part, own, got,
+    snd_t, snd_g, rcv_t, rcv_g, xs, gs, p1, p2, e_snd, e_all, c_snd, c_all, l_snd, l_all,
+    out_r, out_d, ret_r, ret_d, part, own, got, part_c, own_c, got_c,
     ld_sem, t_ss, t_rs, g_ss, g_rs, r_ss, r_rs, d_ss, d_rs,
-    e_ss, e_rs, l_ss, l_rs, w_ss, w_rs, here,
+    e_ss, e_rs, l_ss, l_rs, w_ss, w_rs, c_ss, c_rs, v_ss, v_rs, here,
 ):
     dp, ex = lax.axis_index("dp"), lax.axis_index("expert")
     y, z = lax.rem(dp, 8), lax.div(dp, 8)
@@ -196,6 +196,7 @@
         )
 
     eset, lset = (e_snd, e_all, e_ss, e_rs), (l_snd, l_all, l_ss, l_rs)
+    cset = (c_snd, c_all, c_ss, c_rs)
 
     def take(group, kind, buf):
         for slot in range(4 * group + 3, 4 * group - 1, -1):
@@ -205,14 +206,16 @@
         for b in range(BLOCKS):
             buf[rows(group, MSG), b * CUT:(b + 1) * CUT] = turned[b * MSG:(b + 1) * MSG, :]
 
-    def spill(half, classes, width, values, kind):
+    def spill(half, classes, values, kind):
+        low = 256 if classes else 0
         for m in (3, 2, 1, 0):
             buf = kind[0] if m else kind[1]
             place = pl.ds(GROUP * (m - 1) + half * HALF if m else 4 * half * HALF, HALF)
-            buf[place, 0:128] = classes[m][0]
-            buf[place, 128:256] = classes[m][1]
+            if classes:
+                buf[place, 0:128] = classes[m][0]
+                buf[place, 128:256] = classes[m][1]
             for i, value in enumerate(values):
-                buf[place, 256 + i * width:256 + (i + 1) * width] = value
+                buf[place, low + i * 384:low + (i + 1) * 384] = value
             if m:
                 for group in (2 * half + 1, 2 * half):
                     forward(group, m, *kind).start()
@@ -225,12 +228,13 @@
         silu = a * s
         p1[at, :] = u * s * (1.0 + a * (1.0 - s))
         p2[at, :] = silu
-        spill(half, pack(xs, at), 384, [(silu * u).astype(BF16)], eset)
+        spill(half, pack(xs, at), [(silu * u).astype(BF16)], eset)
 
     def late(half):
         at = rows(half, HALF)
+        spill(half, pack(gs, at), [], cset)
         d_act = dot(gs[at, :], down[...], NT)
-        spill(half, pack(gs, at), 384, [(d_act * p1[at, :]).astype(BF16), (d_act * p2[at, :]).astype(BF16)], lset)
+        spill(half, None, [(d_act * p1[at, :]).astype(BF16), (d_act * p2[at, :]).astype(BF16)], lset)
 
     def give(value, kind):
         buf = kind[0]
@@ -268,40 +272,48 @@
     take(1, gset, gs)
     take(0, gset, gs)
     late(0)
-    give(dot(mine(l_all, 256, 1024), gu[...], NT).astype(BF16), dset)
-
-    def share(m):
+    give(dot(mine(l_all, 0, 768), gu[...], NT).astype(BF16), dset)
+
+    wset, vset = (part, got, w_ss, w_rs), (part_c, got_c, v_ss, v_rs)
+
+    def share(m, src, dst, ss, rs):
         yy, zz = peer(m)
         other = ((4 - m // 4) % 4) * 4 + (4 - m % 4) % 4
         return pltpu.make_async_remote_copy(
-            part.at[lax.div(zz, 2) * 4 + lax.div(yy, 2)], got.at[other], w_ss.at[m], w_rs.at[other],
+            src.at[lax.div(zz, 2) * 4 + lax.div(yy, 2)], dst.at[other], ss.at[m], rs.at[other],
             device_id=dp_at(yy, zz), device_id_type=MESH,
         )
 
-    def shared(m):
+    def shared(m, src, dst, ss, rs):
         return pltpu.make_async_remote_copy(
-            part.at[m], got.at[m], w_ss.at[m], w_rs.at[m],
+            src.at[m], dst.at[m], ss.at[m], rs.at[m],
             device_id=dp_at(*peer(m)), device_id_type=MESH,
         )
 
-    first = last = 0.0
-    for half in (1, 0):
-        for m in (1, 2, 3):
-            for group in (2 * half + 1, 2 * half):
-                forward(group, m, *eset).wait_recv()
-                forward(group, m, *lset).wait_recv()
-        at = rows(half, 4 * HALF)
-        first = first + dot(e_all[at, 0:256], l_all[at, 256:1024], TN)
-        last = last + dot(l_all[at, 0:256], e_all[at, 256:640], TN)
+    def made_of(kinds, left, right):
+        product = 0.0
+        for half in (1, 0):
+            for m in (1, 2, 3):
+                for group in (2 * half + 1, 2 * half):
+                    for kind in kinds:
+                        forward(group, m, *kind).wait_recv()
+            at = rows(half, 4 * HALF)
+            product = product + dot(left(at), right(at), TN)
+        return product
+
+    def send_blocks(product, kind, kept):
+        for k in range(16):
+            kind[0][k] = product[k * 16:(k + 1) * 16, :].astype(BF16)
+        for m in PEERS:
+            share(m, *kind).start()
+        for k in range(16):
+            kept[k] = product[k * 16:(k + 1) * 16, :]
+
+    last = made_of((eset, cset), lambda at: c_all[at, :], lambda at: e_all[at, 256:640])
     pl.semaphore_wait(here.at[4], 1)
-    for k in range(16):
-        part[k, :, 0:768] = first[k * 16:(k + 1) * 16, :].astype(BF16)
-        part[k, :, 768:1152] = last[k * 16:(k + 1) * 16, :].astype(BF16)
-    for m in PEERS:
-        share(m).start()
-    for k in range(16):
-        own[k, :, 0:768] = first[k * 16:(k + 1) * 16, :]
-        own[k, :, 768:1152] = last[k * 16:(k + 1) * 16, :]
+    send_blocks(last, vset, own_c)
+    first = made_of((lset,), lambda at: e_all[at, 0:256], lambda at: l_all[at, :])
+    send_blocks(first, wset, own)
 
     ret_r[0:MSG, :] = out_r[0:MSG, :]
     ret_d[0:MSG, :] = out_d[0:MSG, :]
@@ -318,19 +330,22 @@
     for b in range(BLOCKS):
         tgrad_ref[:, b * CUT:(b + 1) * CUT] = dot(gather[rows(b, 128), :], ret_d[...]).astype(BF16)
 
-    total = own[lax.div(z, 2) * 4 + lax.div(y, 2)]
-    for m in range(1, 16):
-        shared(m).wait_recv()
-        total = total + got[m].astype(F32)
-    wgrad_ref[0] = total
+    mine_at = lax.div(z, 2) * 4 + lax.div(y, 2)
+    for kind, kept, low, high in ((vset, own_c, 768, 1152), (wset, own, 0, 768)):
+        total = kept[mine_at]
+        for m in range(1, 16):
+            shared(m, *kind).wait_recv()
+            total = total + kind[1][m].astype(F32)
+        wgrad_ref[0, :, low:high] = total
 
     for slot in range(1, 16):
         for kind in (tset, gset, rset, dset):
             exchange(slot, *kind).wait_send()
-        share(slot).wait_send()
+        share(slot, *vset).wait_send()
+        share(slot, *wset).wait_send()
     for group in range(4):
         for m in (1, 2, 3):
-            for kind in (eset, lset):
+            for kind in (eset, cset, lset):
                 forward(group, m, *kind).wait_send()
 
 
@@ -360,11 +375,14 @@
         pltpu.VMEM((GROUP, width), BF16), pltpu.VMEM((GROUP, width), BF16),
         pltpu.VMEM((GROUP, hidden), F32), pltpu.VMEM((GROUP, hidden), F32),
         pltpu.VMEM((3 * GROUP, 256 + hidden), BF16), pltpu.VMEM((4 * GROUP, 256 + hidden), BF16),
-        pltpu.VMEM((3 * GROUP, 256 + 2 * hidden), BF16), pltpu.VMEM((4 * GROUP, 256 + 2 * hidden), BF16),
+        pltpu.VMEM((3 * GROUP, 256), BF16), pltpu.VMEM((4 * GROUP, 256), BF16),
+        pltpu.VMEM((3 * GROUP, 2 * hidden), BF16), pltpu.VMEM((4 * GROUP, 2 * hidden), BF16),
         *[pltpu.VMEM((slots, CUT), BF16)] * 4,
-        pltpu.VMEM((16, 16, 3 * hidden), BF16), pltpu.VMEM((16, 16, 3 * hidden), F32),
-        pltpu.VMEM((16, 16, 3 * hidden), BF16),
-        dma((12,)), *[dma((16,))] * 14,
+        pltpu.VMEM((16, 16, 2 * hidden), BF16), pltpu.VMEM((16, 16, 2 * hidden), F32),
+        pltpu.VMEM((16, 16, 2 * hidden), BF16),
+        pltpu.VMEM((16, 16, hidden), BF16), pltpu.VMEM((16, 16, hidden), F32),
+        pltpu.VMEM((16, 16, hidden), BF16),
+        dma((12,)), *[dma((16,))] * 18,
         pltpu.SemaphoreType.REGULAR((5,)),
     ]
     outs = (

time: 73.4 us -> 73.2 us (level)
  the two profiles are of different devices: /device:TPU:1 before, /device:TPU:5 now
where the time goes in v4:
time: 73.2 us; the launch traced here: 73 us
  Pallas kernels  72.3 us (99%)
    pallas_call x1, Pallas kernels, on_device(): pl.pallas_call(kernel, out_shape=tuple((pltpu.VMEM(o.shape, o.dtype) for...  71.5 us

profile of v4, /device:TPU:5, one launch (start us, length us, event | category | flops | bytes accessed | tf_op | source)
XLA Modules:
  0.0 73.0 jit_solution(5355199276985528644)
XLA Ops:
  0.6 71.5 %shard_map.93 = (bf16[128,1024]{1,0:T(8,128)(2,1)S(1)}, bf16[128,1024]{1,0:T(8,128)(2,1)S(1)}, f32[1,128]{1,0:T(1,128)S(1)}, f32[1,16,1152]{2,1,0:T(8,128)S(1)}) custom-call(s32[1,128]{1,0:T(1,128)} %bitcast.3, f32[1,128]{1,0:T(1,128)} %bitcast.4, bf16[128,1024]{1,0:T(8,128)(2,1)} %tok_hbm.1, bf16[128,1024]{1,0:T(8,128)(2,1)} %grad_hbm.1, ...), custom_call_target="tpu_custom_call" | custom-call | tf_op jit(solution)/shard_map/pallas_call | solution.py:394
  72.1 0.8 %shard_map.94 = (bf16[128,1024]{1,0:T(8,128)(2,1)}, bf16[128,1024]{1,0:T(8,128)(2,1)}, f32[1,128]{1,0:T(1,128)}, f32[1,16,1152]{2,1,0:T(8,128)}) custom-call(bf16[128,1024]{1,0:T(8,128)(2,1)S(1)} %get-tuple-element.12.refs_0_, bf16[128,1024]{1,0:T(8,128)(2,1)S(1)} %get-tuple-element.13.refs_1_, f32[1,128]{1,0:T(1,128)S(1)} %get-tuple-element.14.refs_2_, ...), custom_call_target="tpu_custom_call" | custom-call | tf_op jit(solution)/shard_map/pallas_call | solution.py:404

commit v5 on v4

--- a/solution.py
+++ b/solution.py
@@ -330,23 +330,26 @@
     for b in range(BLOCKS):
         tgrad_ref[:, b * CUT:(b + 1) * CUT] = dot(gather[rows(b, 128), :], ret_d[...]).astype(BF16)
 
+    for slot in range(1, 16):
+        for kind in (tset, gset, rset, dset):
+            exchange(slot, *kind).wait_send()
+    for group in range(4):
+        for m in (1, 2, 3):
+            for kind in (eset, cset, lset):
+                forward(group, m, *kind).wait_send()
+    for slot in range(1, 16):
+        share(slot, *vset).wait_send()
+
     mine_at = lax.div(z, 2) * 4 + lax.div(y, 2)
     for kind, kept, low, high in ((vset, own_c, 768, 1152), (wset, own, 0, 768)):
         total = kept[mine_at]
+        if kind is wset:
+            for m in range(1, 16):
+                share(m, *wset).wait_send()
         for m in range(1, 16):
             shared(m, *kind).wait_recv()
             total = total + kind[1][m].astype(F32)
         wgrad_ref[0, :, low:high] = total
-
-    for slot in range(1, 16):
-        for kind in (tset, gset, rset, dset):
-            exchange(slot, *kind).wait_send()
-        share(slot, *vset).wait_send()
-        share(slot, *wset).wait_send()
-    for group in range(4):
-        for m in (1, 2, 3):
-            for kind in (eset, cset, lset):
-                forward(group, m, *kind).wait_send()
 
 
 def hand_over(*refs):

time: 73.2 us -> 73 us (level)
  no operation moved by 1% of the time
where the time goes in v5:
time: 73 us; the launch traced here: 72.8 us
  Pallas kernels  72.1 us (99%)
    pallas_call x1, Pallas kernels, on_device(): pl.pallas_call(kernel, out_shape=tuple((pltpu.VMEM(o.shape, o.dtype) for...  71.3 us

profile of v5, /device:TPU:5, one launch (start us, length us, event | category | flops | bytes accessed | tf_op | source)
XLA Modules:
  0.0 72.8 jit_solution(17837943542421316995)
XLA Ops:
  0.6 71.3 %shard_map.93 = (bf16[128,1024]{1,0:T(8,128)(2,1)S(1)}, bf16[128,1024]{1,0:T(8,128)(2,1)S(1)}, f32[1,128]{1,0:T(1,128)S(1)}, f32[1,16,1152]{2,1,0:T(8,128)S(1)}) custom-call(s32[1,128]{1,0:T(1,128)} %bitcast.3, f32[1,128]{1,0:T(1,128)} %bitcast.4, bf16[128,1024]{1,0:T(8,128)(2,1)} %tok_hbm.1, bf16[128,1024]{1,0:T(8,128)(2,1)} %grad_hbm.1, ...), custom_call_target="tpu_custom_call" | custom-call | tf_op jit(solution)/shard_map/pallas_call | solution.py:397
  71.9 0.8 %shard_map.94 = (bf16[128,1024]{1,0:T(8,128)(2,1)}, bf16[128,1024]{1,0:T(8,128)(2,1)}, f32[1,128]{1,0:T(1,128)}, f32[1,16,1152]{2,1,0:T(8,128)}) custom-call(bf16[128,1024]{1,0:T(8,128)(2,1)S(1)} %get-tuple-element.12.refs_0_, bf16[128,1024]{1,0:T(8,128)(2,1)S(1)} %get-tuple-element.13.refs_1_, f32[1,128]{1,0:T(1,128)S(1)} %get-tuple-element.14.refs_2_, ...), custom_call_target="tpu_custom_call" | custom-call | tf_op jit(solution)/shard_map/pallas_call | solution.py:407
